TPU v7x, 128 devices: a whole 4x4x4 slice. The times are simulated.
128 devices in a mesh: dp: 8 (over z, core), expert: 16 (over y, x).
Axes of the slice: x: 4, y: 4, z: 4, core: 2. Of those that a mesh axis runs over, the one named last changes fastest.
Arguments:
- tokens: bfloat16 [16384, 4096], P(('dp', 'expert')), may hold values from -6 to 6
- routes: int32 [16384, 2], P(('dp', 'expert')), may hold values from 0 to 15, all different within a row; in each aligned block of 128 rows (0 to 127, 128 to 255, ...) at most 24 rows name the same one
- gates: float32 [16384, 2], P(('dp', 'expert')), may hold values from 0.1 to 1
- cotangent: bfloat16 [16384, 4096], P(('dp', 'expert')), may hold values from -6 to 6
- w_gate: bfloat16 [16, 4096, 768], P('expert'), may hold values from -0.09375 to 0.09375
- w_up: bfloat16 [16, 4096, 768], P('expert'), may hold values from -0.09375 to 0.09375
- w_down: bfloat16 [16, 768, 4096], P('expert'), may hold values from -0.21875 to 0.21875
Outputs:
- mixed: bfloat16 [16384, 4096], P(('dp', 'expert'))
- grad_tokens: bfloat16 [16384, 4096], P(('dp', 'expert'))
- grad_gates: float32 [16384, 2], P(('dp', 'expert'))
- grad_w_gate: bfloat16 [16, 4096, 768], P('expert', 'dp')
- grad_w_up: bfloat16 [16, 4096, 768], P('expert', 'dp')
- grad_w_down: bfloat16 [16, 768, 4096], P('expert', 'dp')
Inputs may be any that keep to these rules, and one draw needn't show every extreme that they name: `routes`: each token names 2 different experts; in the 128 rows of one device no expert is named more than 24 times, a bound that some block reaches.
All inputs are finite; a program needn't handle non-finite values.
Results may differ from a plain program's by a relative error of at most 0.017.
Values may be sent and summed in bfloat16 or wider, within the bound.
A program may use at most 128 MiB of HBM per device.

v0:
```python
import jax
import jax.numpy as jnp
from jax import lax
from jax.sharding import PartitionSpec as P


def slot_select(routes, experts, capacity):
    toks, top = routes.shape
    flat = routes.reshape(-1)
    onehot = (flat[:, None] == jnp.arange(experts, dtype=jnp.int32)[None, :]).astype(jnp.int32)
    before = jnp.cumsum(onehot, axis=0) - onehot
    position = jnp.sum(before * onehot, axis=1)
    target = (flat * capacity + position).reshape(toks, top)
    slots = jnp.arange(experts * capacity, dtype=jnp.int32)
    return (target.T[:, None, :] == slots[None, :, None]).astype(jnp.bfloat16)


def contract_rows(left, right):
    return lax.dot_general(
        left, right, (((0,), (0,)), ((), ())), preferred_element_type=jnp.float32
    )


def contract_cols(left, right):
    return lax.dot_general(
        left, right, (((1,), (1,)), ((), ())), preferred_element_type=jnp.float32
    )


def forward_rows(rows_x, wg, wu, wd):
    h_pre = jnp.dot(rows_x, wg, preferred_element_type=jnp.float32)
    u_pre = jnp.dot(rows_x, wu, preferred_element_type=jnp.float32)
    act = (h_pre * jax.nn.sigmoid(h_pre) * u_pre).astype(jnp.bfloat16)
    rows_out = jnp.dot(act, wd, preferred_element_type=jnp.float32).astype(jnp.bfloat16)
    return (rows_out, act, h_pre, u_pre)


def backward_rows(h_pre, u_pre, rows_d, wg, wu, wd):
    sig = jax.nn.sigmoid(h_pre)
    d_act = contract_cols(rows_d, wd)
    d_hid = (d_act * u_pre * sig * (1.0 + h_pre * (1.0 - sig))).astype(jnp.bfloat16)
    d_upv = (d_act * h_pre * sig).astype(jnp.bfloat16)
    rows_dx = (contract_cols(d_hid, wg) + contract_cols(d_upv, wu)).astype(jnp.bfloat16)
    return (d_hid, d_upv, rows_dx)


def per_device(tokens, routes, gates, cotangent, w_gate, w_up, w_down):
    experts = lax.axis_size("expert")
    capacity = routes.shape[0] * routes.shape[1] * 3 // (2 * experts)
    model = tokens.shape[1]
    select = slot_select(routes, experts, capacity)
    slot_rows = experts * capacity
    xbuf = jnp.einsum("krt,td->rd", select, tokens, preferred_element_type=jnp.float32)
    xbuf = xbuf.astype(jnp.bfloat16).reshape(experts, capacity, model)
    cot_wide = cotangent.astype(jnp.float32)
    dpair = (gates[:, :, None] * cot_wide[:, None, :]).astype(jnp.bfloat16)
    dbuf = jnp.einsum("krt,tkd->rd", select, dpair, preferred_element_type=jnp.float32)
    dbuf = dbuf.astype(jnp.bfloat16).reshape(experts, capacity, model)
    wg, wu, wd = (w_gate[0], w_up[0], w_down[0])
    hidden = wg.shape[1]
    x_items = lax.all_to_all(xbuf, "expert", split_axis=0, concat_axis=0, tiled=True)
    count = x_items.shape[1]
    rows_out, act, h_pre, u_pre = forward_rows(x_items.reshape(-1, model), wg, wu, wd)
    back = lax.all_to_all(
        rows_out.reshape(experts, count, model), "expert", split_axis=0, concat_axis=0, tiled=True
    )
    back_out, x_recv, h_pre, u_pre, act = (
        back,
        x_items,
        h_pre.reshape(experts, count, hidden),
        u_pre.reshape(experts, count, hidden),
        act.reshape(experts, count, hidden),
    )
    d_recv = lax.all_to_all(dbuf, "expert", split_axis=0, concat_axis=0, tiled=True)
    rows_x = x_recv.reshape(-1, model)
    rows_d = d_recv.reshape(-1, model)
    act = act.reshape(-1, hidden)
    d_hid, d_upv, rows_dx = backward_rows(
        h_pre.reshape(-1, hidden), u_pre.reshape(-1, hidden), rows_d, wg, wu, wd
    )
    back_dx = lax.all_to_all(
        rows_dx.reshape(experts, capacity, model), "expert", split_axis=0, concat_axis=0, tiled=True
    )
    grad_g, grad_u, grad_d = (
        lax.psum_scatter(
            contract_rows(rows_x, d_hid).astype(jnp.bfloat16), "dp", scatter_dimension=0, tiled=True
        ).astype(jnp.float32),
        lax.psum_scatter(
            contract_rows(rows_x, d_upv).astype(jnp.bfloat16), "dp", scatter_dimension=0, tiled=True
        ).astype(jnp.float32),
        lax.psum_scatter(
            contract_rows(act, rows_d).astype(jnp.bfloat16), "dp", scatter_dimension=0, tiled=True
        ).astype(jnp.float32),
    )
    out_pair = jnp.einsum(
        "krt,rd->tkd",
        select,
        back_out.reshape(slot_rows, model),
        preferred_element_type=jnp.float32,
    )
    mixed = jnp.sum(gates[:, :, None] * out_pair, axis=1).astype(jnp.bfloat16)
    grad_gates = jnp.sum(cot_wide[:, None, :] * out_pair, axis=2)
    grad_tokens = jnp.einsum(
        "krt,rd->td", select, back_dx.reshape(slot_rows, model), preferred_element_type=jnp.float32
    ).astype(jnp.bfloat16)
    return (
        mixed,
        grad_tokens,
        grad_gates,
        grad_g.astype(jnp.bfloat16)[None],
        grad_u.astype(jnp.bfloat16)[None],
        grad_d.astype(jnp.bfloat16)[None],
    )


def solution(mesh):
    placed = (
        P(("dp", "expert"), None),
        P(("dp", "expert"), None),
        P(("dp", "expert"), None),
        P(("dp", "expert"), None),
        P("expert", None, None),
        P("expert", None, None),
        P("expert", None, None),
    )
    return jax.shard_map(
        per_device,
        mesh=mesh,
        in_specs=placed,
        out_specs=(
            P(("dp", "expert"), None),
            P(("dp", "expert"), None),
            P(("dp", "expert"), None),
            P("expert", "dp", None),
            P("expert", "dp", None),
            P("expert", "dp", None),
        ),
        check_vma=False,
    )
```

profile of v0, /device:TPU:0, one launch (start us, length us, event | category | flops | bytes accessed | tf_op | source)
XLA Modules:
  0.0 280.0 jit_solution(6899729867418116095)
XLA Ops:
  7.2 0.0 copy-start
  7.2 0.0 copy-start.2
  7.2 0.9 copy.35
  8.1 0.1 eq.42
  8.2 0.1 eq.38
  8.4 0.6 reduce-window.6
  9.0 0.2 slice_reduce_fusion
  9.2 0.1 fusion.24
  9.3 0.1 reduce_sum.43
  9.4 0.1 copy.38
  9.5 0.7 add_bitcast_fusion.1
  10.2 1.5 copy.40
  11.7 0.0 copy-done.2
  11.7 2.7 bitcast_convert_fusion
  14.4 7.2 %all-to-all-start.2 = ((bf16[16,24,4096]{2,1,0:T(8,128)(2,1)}), bf16[16,24,4096]{2,1,0:T(8,128)(2,1)}, u32[]{:S(2)}, u32[]{:S(2)}) async-start(bf16[16,24,4096]{2,1,0:T(8,128)(2,1)} %bitcast.77), calls=%async_computation.2 | async-start | bytes 6291456 | tf_op jit(solution)/shard_map/all_to_all | solution.py:74
  21.6 0.0 copy-done
  21.6 2.6 fusion.26
  24.3 44.9 %all-to-all-done.2 = bf16[16,24,4096]{2,1,0:T(8,128)(2,1)} async-done(((bf16[16,24,4096]{2,1,0:T(8,128)(2,1)}), bf16[16,24,4096]{2,1,0:T(8,128)(2,1)}, u32[]{:S(2)}, u32[]{:S(2)}) %all-to-all-start.2) | async-done | bytes 3145760 | tf_op jit(solution)/shard_map/all_to_all | solution.py:74
  69.2 4.5 %all-to-all-start = ((bf16[16,24,4096]{2,1,0:T(8,128)(2,1)}), bf16[16,24,4096]{2,1,0:T(8,128)(2,1)}, u32[]{:S(2)}, u32[]{:S(2)}) async-start(bf16[16,24,4096]{2,1,0:T(8,128)(2,1)} %bitcast.76), calls=%async_computation | async-start | bytes 6291456 | tf_op jit(solution)/shard_map/all_to_all | solution.py:61
  73.6 0.0 reduce-scatter.8.cloned.1.call-start
  73.7 7.4 %fusion = f32[384,768]{1,0:T(8,128)} fusion(bf16[384,4096]{1,0:T(8,128)(2,1)} %bitcast.13, bf16[1,768,4096]{2,1,0:T(8,128)(2,1)} %param.13), kind=kOutput, calls=%fused_computation.4 | convolution fusion | flops 2415919104 | bytes 10616832 | tf_op jit(solution)/shard_map/dot_general | solution.py:25
  81.1 37.5 %all-to-all-done = bf16[16,24,4096]{2,1,0:T(8,128)(2,1)} async-done(((bf16[16,24,4096]{2,1,0:T(8,128)(2,1)}), bf16[16,24,4096]{2,1,0:T(8,128)(2,1)}, u32[]{:S(2)}, u32[]{:S(2)}) %all-to-all-start) | async-done | bytes 3145760 | tf_op jit(solution)/shard_map/all_to_all | solution.py:61
  118.6 0.0 copy-start.5
  118.6 6.4 %fusion.6 = f32[384,768]{1,0:T(8,128)S(1)} fusion(bf16[384,4096]{1,0:T(8,128)(2,1)} %bitcast.3, bf16[1,4096,768]{2,1,0:T(8,128)(2,1)} %param.12), kind=kOutput, calls=%fused_computation.10 | convolution fusion | flops 2415919104 | bytes 10616832 | tf_op jit(solution)/shard_map/dot_general | solution.py:32
  125.0 0.0 copy-done.5
  125.0 7.5 %multiply_convert_fusion.3 = (bf16[384,768]{1,0:T(8,128)(2,1)}, bf16[384,768]{1,0:T(8,128)(2,1)S(1)}, bf16[384,768]{1,0:T(8,128)(2,1)S(1)}) fusion(f32[384,768]{1,0:T(8,128)S(1)} %copy-done.5, f32[384,768]{1,0:T(8,128)S(1)} %fusion.6, bf16[384,4096]{1,0:T(8,128)(2,1)} %bitcast.3, bf16[1,4096,768]{2,1,0:T(8,128)(2,1)} %param.11), kind=kOutput, calls=%fused_computation.27 | convolution fusion | flops 2420637696 | bytes 13565952 | tf_op jit(solution)/shard_map/dot_general | solution.py:31
  132.5 0.0 copy-start.3
  132.5 0.8 copy-done.3
  133.3 7.3 %convolution_convert_fusion = bf16[768,4096]{1,0:T(8,128)(2,1)} fusion(bf16[384,768]{1,0:T(8,128)(2,1)S(1)} %get-tuple-element.21, bf16[384,4096]{1,0:T(8,128)(2,1)} %bitcast.13), kind=kOutput, calls=%fused_computation | convolution fusion | flops 2419064832 | bytes 10027008 | tf_op jit(solution)/shard_map/dot_general | solution.py:19
  140.6 0.0 reduce-scatter.8.cloned.1.call-update
  140.7 0.2 reduce-scatter.4.cloned.1.call-start
  140.9 8.2 %convolution_convert_fusion.2 = bf16[4096,768]{1,0:T(8,128)(2,1)} fusion(bf16[384,4096]{1,0:T(8,128)(2,1)} %bitcast.3, bf16[384,768]{1,0:T(8,128)(2,1)} %get-tuple-element.20), kind=kOutput, calls=%fused_computation.2 | convolution fusion | flops 2419064832 | bytes 10027008 | tf_op jit(solution)/shard_map/dot_general | solution.py:19
  149.1 0.0 reduce-scatter.4.cloned.1.call-update
  149.1 0.0 reduce-scatter.6.cloned.1.call-start
  149.1 8.0 %convolution_convert_fusion.1 = bf16[4096,768]{1,0:T(8,128)(2,1)} fusion(bf16[384,4096]{1,0:T(8,128)(2,1)} %bitcast.3, bf16[384,768]{1,0:T(8,128)(2,1)S(1)} %get-tuple-element.22), kind=kOutput, calls=%fused_computation.1 | convolution fusion | flops 2419064832 | bytes 10027008 | tf_op jit(solution)/shard_map/dot_general | solution.py:19
  157.1 0.0 reduce-scatter.6.cloned.1.call-update
  157.1 7.5 %fusion.14 = bf16[384,4096]{1,0:T(8,128)(2,1)} fusion(bf16[384,768]{1,0:T(8,128)(2,1)} %copy-done.3, bf16[1,768,4096]{2,1,0:T(8,128)(2,1)} %param.13), kind=kOutput, calls=%fused_computation.17 | convolution fusion | flops 2417491968 | bytes 10027008 | tf_op jit(solution)/shard_map/dot_general | solution.py:34
  164.6 4.5 %all-to-all-start.1 = ((bf16[16,24,4096]{2,1,0:T(8,128)(2,1)}), bf16[16,24,4096]{2,1,0:T(8,128)(2,1)}, u32[]{:S(2)}, u32[]{:S(2)}) async-start(bf16[16,24,4096]{2,1,0:T(8,128)(2,1)} %bitcast.79), calls=%async_computation.1 | async-start | bytes 6291456 | tf_op jit(solution)/shard_map/all_to_all | solution.py:64
  169.1 0.0 copy-start.4
  169.1 4.9 %fusion.4 = f32[384,4096]{1,0:T(8,128)S(1)} fusion(bf16[384,768]{1,0:T(8,128)(2,1)S(1)} %get-tuple-element.22, bf16[1,4096,768]{2,1,0:T(8,128)(2,1)} %param.12), kind=kOutput, calls=%fused_computation.8 | convolution fusion | flops 2415919104 | bytes 13172736 | tf_op jit(solution)/shard_map/dot_general | solution.py:25
  174.0 0.0 copy-done.4
  174.1 8.5 %add_convert_fusion = bf16[384,4096]{1,0:T(8,128)(2,1)} fusion(f32[384,4096]{1,0:T(8,128)S(1)} %fusion.4, bf16[384,768]{1,0:T(8,128)(2,1)S(1)} %copy-done.4, bf16[1,4096,768]{2,1,0:T(8,128)(2,1)} %param.11), kind=kOutput, calls=%fused_computation.16 | convolution fusion | flops 2419064832 | bytes 16318464 | tf_op jit(solution)/shard_map/dot_general | solution.py:25
  182.6 29.1 %all-to-all-done.1 = bf16[16,24,4096]{2,1,0:T(8,128)(2,1)} async-done(((bf16[16,24,4096]{2,1,0:T(8,128)(2,1)}), bf16[16,24,4096]{2,1,0:T(8,128)(2,1)}, u32[]{:S(2)}, u32[]{:S(2)}) %all-to-all-start.1) | async-done | bytes 3145760 | tf_op jit(solution)/shard_map/all_to_all | solution.py:64
  211.7 4.7 %all-to-all-start.3 = ((bf16[16,24,4096]{2,1,0:T(8,128)(2,1)}), bf16[16,24,4096]{2,1,0:T(8,128)(2,1)}, u32[]{:S(2)}, u32[]{:S(2)}) async-start(bf16[16,24,4096]{2,1,0:T(8,128)(2,1)} %bitcast.78), calls=%async_computation.3 | async-start | bytes 6291456 | tf_op jit(solution)/shard_map/all_to_all | solution.py:81
  216.4 4.5 %multiply_reduce_fusion = (f32[128,2]{0,1:T(2,128)}, bf16[128,4096]{0,1:T(8,128)(2,1)}) fusion(f32[128,4096]{0,1:T(8,128)S(1)} %copy.40, f32[128,2]{0,1:T(2,128)S(1)} %copy-done.2, bf16[384,4096,1]{1,0,2:T(8,128)(2,1)} %bitcast.9, s32[2,128]{1,0:T(2,128)S(1)} %add_bitcast_fusion.1), kind=kOutput, calls=%fused_computation.21 | convolution fusion | flops 809074432 | bytes 6294528 | tf_op jit(solution)/shard_map/krt,rd->tkd/dot_general | solution.py:95
  220.9 0.0 copy-start.1
  220.9 2.4 copy.42
  223.2 36.3 %all-to-all-done.3 = bf16[16,24,4096]{2,1,0:T(8,128)(2,1)} async-done(((bf16[16,24,4096]{2,1,0:T(8,128)(2,1)}), bf16[16,24,4096]{2,1,0:T(8,128)(2,1)}, u32[]{:S(2)}, u32[]{:S(2)}) %all-to-all-start.3) | async-done | bytes 3145760 | tf_op jit(solution)/shard_map/all_to_all | solution.py:81
  259.6 3.7 %fusion.27 = bf16[128,4096]{1,0:T(8,128)(2,1)} fusion(bf16[384,128]{1,0:T(8,128)(2,1)S(1)} %convert_reduce_fusion, bf16[384,4096]{1,0:T(8,128)(2,1)} %bitcast.15), kind=kOutput, calls=%fused_computation.46 | convolution fusion | flops 402653184 | bytes 4292608 | tf_op jit(solution)/shard_map/krt,rd->td/dot_general | solution.py:103
  263.2 0.0 reduce-scatter.8.cloned.1.call-done
  263.2 0.0 reduce-scatter.4.cloned.1.call-done
  263.3 10.2 %reduce-scatter.6.cloned.1.call-done = bf16[512,768]{1,0:T(8,128)(2,1)} async-done(((bf16[4096,768]{1,0:T(8,128)(2,1)}), bf16[512,768]{1,0:T(8,128)(2,1)}) %reduce-scatter.6.cloned.1.call-update) | async-done | bytes 786448 | tf_op jit(solution)/shard_map/reduce_scatter | solution.py:88
  273.5 0.0 copy-done.1
  (4 shorter events, 0.1 us)
Async XLA Ops:
  7.2 14.5 %copy-start = (bf16[128,4096]{1,0:T(8,128)(2,1)S(1)}, bf16[128,4096]{1,0:T(8,128)(2,1)}, u32[]{:S(2)}) copy-start(bf16[128,4096]{1,0:T(8,128)(2,1)} %param.7) | copy-start | bytes 3145732
  7.2 4.5 %copy-start.2 = (f32[128,2]{0,1:T(2,128)S(1)}, f32[128,2]{0,1:T(2,128)}, u32[]{:S(2)}) copy-start(f32[128,2]{0,1:T(2,128)} %param.9) | copy-start | bytes 3076
  14.4 54.7 %all-to-all-start.2 = ((bf16[16,24,4096]{2,1,0:T(8,128)(2,1)}), bf16[16,24,4096]{2,1,0:T(8,128)(2,1)}, u32[]{:S(2)}, u32[]{:S(2)}) async-start(bf16[16,24,4096]{2,1,0:T(8,128)(2,1)} %bitcast.77), calls=%async_computation.2 | async-start | bytes 6291456 | tf_op jit(solution)/shard_map/all_to_all | solution.py:74
  69.2 49.4 %all-to-all-start = ((bf16[16,24,4096]{2,1,0:T(8,128)(2,1)}), bf16[16,24,4096]{2,1,0:T(8,128)(2,1)}, u32[]{:S(2)}, u32[]{:S(2)}) async-start(bf16[16,24,4096]{2,1,0:T(8,128)(2,1)} %bitcast.76), calls=%async_computation | async-start | bytes 6291456 | tf_op jit(solution)/shard_map/all_to_all | solution.py:61
  73.6 189.6 %reduce-scatter.8.cloned.1.call-start = ((), (), s32[]{:S(2)}) async-start(), calls=%async_computation.9 | async-start | bytes 7077888 | tf_op jit(solution)/shard_map/reduce_scatter | solution.py:91
  118.6 6.4 %copy-start.5 = (f32[384,768]{1,0:T(8,128)S(1)}, f32[384,768]{1,0:T(8,128)}, u32[]{:S(2)}) copy-start(f32[384,768]{1,0:T(8,128)} %fusion) | copy-start | bytes 3538948
  132.5 0.8 copy-start.3
  140.7 122.6 %reduce-scatter.4.cloned.1.call-start = ((), (), s32[]{:S(2)}) async-start(), calls=%async_computation.7 | async-start | bytes 7077888 | tf_op jit(solution)/shard_map/reduce_scatter | solution.py:85
  149.1 124.4 %reduce-scatter.6.cloned.1.call-start = ((), (), s32[]{:S(2)}) async-start(), calls=%async_computation.8 | async-start | bytes 7077888 | tf_op jit(solution)/shard_map/reduce_scatter | solution.py:88
  164.6 47.0 %all-to-all-start.1 = ((bf16[16,24,4096]{2,1,0:T(8,128)(2,1)}), bf16[16,24,4096]{2,1,0:T(8,128)(2,1)}, u32[]{:S(2)}, u32[]{:S(2)}) async-start(bf16[16,24,4096]{2,1,0:T(8,128)(2,1)} %bitcast.79), calls=%async_computation.1 | async-start | bytes 6291456 | tf_op jit(solution)/shard_map/all_to_all | solution.py:64
  169.1 4.9 %copy-start.4 = (bf16[384,768]{1,0:T(8,128)(2,1)S(1)}, bf16[384,768]{1,0:T(8,128)(2,1)}, u32[]{:S(2)}) copy-start(bf16[384,768]{1,0:T(8,128)(2,1)} %get-tuple-element.20) | copy-start | bytes 1769476
  211.7 47.9 %all-to-all-start.3 = ((bf16[16,24,4096]{2,1,0:T(8,128)(2,1)}), bf16[16,24,4096]{2,1,0:T(8,128)(2,1)}, u32[]{:S(2)}, u32[]{:S(2)}) async-start(bf16[16,24,4096]{2,1,0:T(8,128)(2,1)} %bitcast.78), calls=%async_computation.3 | async-start | bytes 6291456 | tf_op jit(solution)/shard_map/all_to_all | solution.py:81
  220.9 52.6 %copy-start.1 = (bf16[128,4096]{1,0:T(8,128)(2,1)S(1)}, bf16[128,4096]{1,0:T(8,128)(2,1)}, u32[]{:S(2)}) copy-start(bf16[128,4096]{1,0:T(8,128)(2,1)} %param.7) | copy-start | bytes 3145732
Sparse Core Ops, SparseCore 0:
  140.8 41.3 reduce-scatter.7
  185.1 42.6 reduce-scatter.3
  230.9 42.5 reduce-scatter.5
where the time goes:
time: 281 us; the launch traced here: 280 us
  waiting for transfers between devices  158 us (56%)
  matrix products  79.2 us (28%)
  starting transfers between devices  21.2 us (8%)
  between operations  13.9 us (5%)
  local copies, waits for them, and re-layouts  6.23 us (2%)
    all_to_all x1, waiting for transfers between devices, per_device(): lax.all_to_all(dbuf, 'expert', split_axis=0, concat_axis=0, tiled=True)  44.9 us
    all_to_all x1, waiting for transfers between devices, per_device(): lax.all_to_all(xbuf, 'expert', split_axis=0, concat_axis=0, tiled=True)  37.5 us
    all_to_all x1, waiting for transfers between devices, per_device(): lax.all_to_all(rows_dx.reshape(experts, capacity, model), 'expert', split...  36.3 us
    all_to_all x1, waiting for transfers between devices, per_device(): lax.all_to_all(rows_out.reshape(experts, count, model), 'expert', split_a...  29.1 us
    dot_general x3, matrix products, contract_rows(): lax.dot_general(left, right, (((0,), (0,)), ((), ())), preferred_element_...  23.4 us
    dot_general x3, matrix products, contract_cols(): lax.dot_general(left, right, (((1,), (1,)), ((), ())), preferred_element_...  20.8 us
    reduce_scatter x1, waiting for transfers between devices, per_device(): lax.psum_scatter(contract_rows(rows_x, d_upv).astype(jnp.bfloat16), 'dp',...  10.2 us
    dot_general x1, matrix products, forward_rows(): h_pre = jnp.dot(rows_x, wg, preferred_element_type=jnp.float32)  7.54 us
  transfers between devices with their start and end apart: 7, of which 5 were waited for; matrix products, arithmetic and copies ran while one was open for 21% of the time, Pallas kernels for 0%

commit v1 on v0

v1 whole, which is shorter than its diff:
```python
import jax
import jax.numpy as jnp
from jax import lax
from jax.experimental import pallas as pl
from jax.experimental.pallas import tpu as pltpu
from jax.sharding import PartitionSpec as P

MESH = pl.DeviceIdType.MESH
F32, BF16 = jnp.float32, jnp.bfloat16
SIDE = 4
GROUPS = (
    ((2, 1), (2, 3), (0, 1), (0, 3)),
    ((1, 2), (3, 2), (1, 0), (3, 0)),
    ((2, 2),),
    ((0, 2), (2, 0)),
    ((1, 1), (3, 3)),
    ((1, 3), (3, 1)),
)
SHIFTS = tuple(shift for group in GROUPS for shift in group)
X, DY, OUT, DX = range(4)


def nn(a, b):
    return lax.dot_general(a, b, (((1,), (0,)), ((), ())), preferred_element_type=F32)


def nt(a, b):
    return lax.dot_general(a, b, (((1,), (1,)), ((), ())), preferred_element_type=F32)


def tn(a, b):
    return lax.dot_general(a, b, (((0,), (0,)), ((), ())), preferred_element_type=F32)


def kernel(
    routes, gates, tok_in, cot_in, wg_in, wu_in, wd_in,
    mixed, grad_tok, grad_gates, grad_g, grad_u, grad_d, out_back,
    tok, cot, wg, wu, wd, sel, sel_t, buf_a, buf_b, xr, dd, xs, h, u, act, dhc, duc, act_t, act_s, dwg, dwu,
    zr_g, zr_u, zr_d, gg,
    send, recv, local, sib_send, sib_recv, z_send, z_recv, load, store, credit,
):
    n_exp, cap, model = buf_a.shape
    rows = n_exp * cap
    hidden = act.shape[1]
    toks = tok.shape[0]
    r, e = lax.axis_index("dp"), lax.axis_index("expert")
    z, c = r // 2, r % 2
    y, x = e // SIDE, e % SIDE

    def peer(shift, sign=1):
        dy, dx = shift
        return (y + sign * dy + SIDE) % SIDE * SIDE + (x + sign * dx + SIDE) % SIDE

    sibling = (r + 1 - 2 * c, e)
    z_up, z_down, z_far = (z + 1) % SIDE, (z + 3) % SIDE, (z + 2) % SIDE
    up, down = (z_up * 2 + c, e), (z_down * 2 + c, e)

    loads = [
        pltpu.make_async_copy(src, dst, load.at[i])
        for i, (src, dst) in enumerate(((tok_in, tok), (cot_in, cot), (wg_in.at[0], wg), (wu_in.at[0], wu), (wd_in.at[0], wd)))
    ]
    for copy in loads:
        copy.start()
    barrier = pltpu.get_barrier_semaphore()
    for shift in SHIFTS:
        pl.semaphore_signal(barrier, inc=1, device_id=(r, peer(shift)), device_id_type=MESH)
    for device in (sibling, up, down):
        pl.semaphore_signal(barrier, inc=1, device_id=device, device_id_type=MESH)

    r0, r1 = routes[0:1, :], routes[1:2, :]
    g0, g1 = gates[0:1, :], gates[1:2, :]
    expert_id = lax.broadcasted_iota(jnp.int32, (n_exp, toks), 0)
    on0, on1 = expert_id == r0, expert_id == r1
    named = jnp.where(on0 | on1, 1.0, 0.0).astype(BF16)
    before = lax.broadcasted_iota(jnp.int32, (toks, toks), 0) < lax.broadcasted_iota(jnp.int32, (toks, toks), 1)
    place = nn(named, jnp.where(before, 1.0, 0.0).astype(BF16))
    s0 = jnp.sum(jnp.where(on0, place, 0.0), axis=0, keepdims=True) + (r0 * cap).astype(F32)
    s1 = jnp.sum(jnp.where(on1, place, 0.0), axis=0, keepdims=True) + (r1 * cap).astype(F32)
    slot = lax.broadcasted_iota(jnp.int32, (rows, toks), 0).astype(F32)
    hit0, hit1 = slot == s0, slot == s1
    sel[...] = jnp.where(hit0 | hit1, 1.0, 0.0).astype(BF16)
    row_gate = jnp.sum(jnp.where(hit0, g0, 0.0) + jnp.where(hit1, g1, 0.0), axis=1, keepdims=True)
    line = lax.broadcasted_iota(jnp.int32, (toks, toks), 0)
    columns = jnp.where(line == 0, s0, jnp.where(line == 1, s1, jnp.where(line == 2, g0, g1))).T
    slot_t = lax.broadcasted_iota(jnp.int32, (toks, rows), 1).astype(F32)
    sel_t[0:toks, :] = jnp.where(slot_t == columns[:, 0:1], 1.0, 0.0).astype(BF16)
    sel_t[toks : 2 * toks, :] = jnp.where(slot_t == columns[:, 1:2], 1.0, 0.0).astype(BF16)
    gate0, gate1 = columns[:, 2:3], columns[:, 3:4]

    def chunks(total, size, body):
        @pl.loop(0, total // size)
        def _(i):
            body(i, pl.ds(pl.multiple_of(i * size, size), size))

    source = (buf_a, buf_b, buf_a, buf_b)
    target = (xr, dd, out_back, xr)

    def block(kind, i):
        to = peer(SHIFTS[i])
        return pltpu.make_async_remote_copy(
            src_ref=source[kind].at[to], dst_ref=target[kind].at[e],
            send_sem=send.at[kind, i], recv_sem=recv.at[kind, i],
            device_id=(r, to), device_id_type=MESH,
        )

    def arriving(kind, i):
        return pltpu.make_async_remote_copy(
            src_ref=source[kind].at[e], dst_ref=target[kind].at[peer(SHIFTS[i], -1)],
            send_sem=send.at[kind, i], recv_sem=recv.at[kind, i],
            device_id=(r, peer(SHIFTS[i])), device_id_type=MESH,
        )

    def own(kind):
        return pltpu.make_async_copy(source[kind].at[e], target[kind].at[e], local.at[kind])

    def begin(kind, after=None):
        own(kind).start()
        first = 0
        for group in GROUPS:
            for i in range(first, first + len(group)):
                if after is not None:
                    block(after, i).wait_send()
            for i in range(first, first + len(group)):
                block(kind, i).start()
            first += len(group)

    def finish(kind):
        own(kind).wait()
        for i in range(len(SHIFTS)):
            arriving(kind, i).wait_recv()

    loads[0].wait()

    def fill_x(_, at):
        buf_a[:, :, at] = nn(sel[...], tok[:, at]).astype(BF16).reshape(n_exp, cap, at.size)

    chunks(model, 1024, fill_x)
    pl.semaphore_wait(barrier, len(SHIFTS) + 3)
    begin(X)
    loads[1].wait()

    def fill_d(_, at):
        buf_b[:, :, at] = (nn(sel[...], cot[:, at]) * row_gate).astype(BF16).reshape(n_exp, cap, at.size)

    chunks(model, 1024, fill_d)
    begin(DY, after=X)

    finish(X)
    part = model // (2 * SIDE)

    def x_part(zz, core):
        return pl.ds(pl.multiple_of((zz * 2 + core) * part, part), part)

    def to_sibling(src, dst, i):
        return pltpu.make_async_remote_copy(
            src_ref=src, dst_ref=dst, send_sem=sib_send.at[i], recv_sem=sib_recv.at[i],
            device_id=sibling, device_id_type=MESH,
        )

    sib_x = [to_sibling(xr.at[:, :, x_part(zz, 1 - c)], xs.at[zz], zz) for zz in range(SIDE)]
    for copy in sib_x:
        copy.start()
    loads[2].wait()
    loads[3].wait()

    def up_proj(_, at):
        full = xr[...].reshape(rows, model)
        hv = nn(full, wg[:, at])
        uv = nn(full, wu[:, at])
        h[:, at] = hv
        u[:, at] = uv
        act[:, at] = (hv * jax.nn.sigmoid(hv) * uv).astype(BF16)

    chunks(hidden, 256, up_proj)
    fslice = hidden // (2 * SIDE)
    for half in range(2):
        piece = act[:, half * SIDE * fslice : (half + 1) * SIDE * fslice].astype(F32).T.astype(BF16)
        for q in range(SIDE):
            index = half * SIDE + q
            act_t[index % 2, index // 2] = piece[q * fslice : (q + 1) * fslice, :]
    sib_act = to_sibling(act_t.at[1 - c], act_s, 4)
    sib_act.start()
    loads[4].wait()

    def down_proj(_, at):
        buf_a[:, :, at] = nn(act[...], wd[:, at]).astype(BF16).reshape(n_exp, cap, at.size)

    chunks(model, 1024, down_proj)
    begin(OUT, after=DY)

    finish(DY)
    sib_d = to_sibling(dd.at[pl.ds(0, n_exp)], dd.at[pl.ds(n_exp, n_exp)], 5)
    sib_d.start()

    def back_act(_, at):
        da = nt(dd[0:n_exp].reshape(rows, model), wd[at, :])
        hv, uv = h[:, at], u[:, at]
        sg = jax.nn.sigmoid(hv)
        dhc[0:rows, at] = (da * uv * sg * (1.0 + hv * (1.0 - sg))).astype(BF16)
        duc[0:rows, at] = (da * hv * sg).astype(BF16)

    chunks(hidden, 256, back_act)
    sib_dh = to_sibling(dhc.at[pl.ds(0, rows)], dhc.at[pl.ds(rows, rows)], 6)
    sib_du = to_sibling(duc.at[pl.ds(0, rows)], duc.at[pl.ds(rows, rows)], 7)
    sib_dh.start()
    sib_du.start()

    sib_act.wait()
    sib_d.wait()

    def grad_down(_, at):
        left = jnp.concatenate([act_t[c].reshape(SIDE * fslice, rows), act_s[...].reshape(SIDE * fslice, rows)], axis=1)
        wd[0 : SIDE * fslice, at] = nn(left, dd[:, :, at].reshape(2 * rows, at.size)).astype(BF16)

    chunks(model, 512, grad_down)

    half_f, half_p = fslice // 2, part // 2

    def half_of(kind, zz, half):
        if kind == 0:
            return wd.at[pl.ds(pl.multiple_of(zz * fslice + half * half_f, half_f), half_f)]
        return (dwg, dwu)[kind - 1].at[zz, pl.ds(half * half_p, half_p)]

    zr = (zr_d, zr_g, zr_u)

    def hop(kind, i, src, device):
        return pltpu.make_async_remote_copy(
            src_ref=src, dst_ref=zr[kind].at[i], send_sem=z_send.at[kind, i], recv_sem=z_recv.at[kind, i],
            device_id=device, device_id_type=MESH,
        )

    def ring(kind, i):
        zz, half = ((z_far, 1), (z_far, 0), (z_up, 0), (z_down, 1), (z_up, 1), (z_down, 0))[i]
        return hop(kind, i, half_of(kind, zz, half), down if i % 2 else up)

    def first_hops(kind):
        for i in range(4):
            ring(kind, i).start()

    def relay(kind):
        for i, zz, half in ((0, z_up, 1), (1, z_down, 0)):
            ring(kind, i).wait_recv()
            mine = half_of(kind, zz, half)
            mine[...] = (mine[...].astype(F32) + zr[kind][i].astype(F32)).astype(BF16)
            ring(kind, i + 4).start()

    def total(kind, out):
        for i in (2, 3, 4, 5):
            ring(kind, i).wait_recv()
        for half, (a, b) in enumerate(((2, 5), (3, 4))):
            mine = half_of(kind, z, half)
            mine[...] = (mine[...].astype(F32) + zr[kind][a].astype(F32) + zr[kind][b].astype(F32)).astype(BF16)
        whole = wd.at[pl.ds(pl.multiple_of(z * fslice, fslice), fslice)] if kind == 0 else (dwg, dwu)[kind - 1].at[z]
        copy = pltpu.make_async_copy(whole, out.at[0], store.at[2 + kind])
        copy.start()
        return copy

    first_hops(0)
    for copy in sib_x:
        copy.wait()

    def grad_in(right, out):
        @pl.loop(0, SIDE)
        def _(i):
            zz = (z + 2 + i) % SIDE
            left = jnp.concatenate([xr[:, :, x_part(zz, c)].reshape(rows, part), xs[zz].reshape(rows, part)], axis=0)
            out[zz] = tn(left, right[...]).astype(BF16)

    sib_dh.wait()
    grad_in(dhc, dwg)
    first_hops(1)
    sib_du.wait()
    grad_in(duc, dwu)
    first_hops(2)
    for i in range(len(SHIFTS)):
        pl.semaphore_signal(credit, inc=1, device_id=(r, peer(SHIFTS[i])), device_id_type=MESH)

    def back_rows(_, at):
        buf_b[:, :, at] = (nt(dhc[0:rows], wg[at, :]) + nt(duc[0:rows], wu[at, :])).astype(BF16).reshape(n_exp, cap, at.size)

    chunks(model, 512, back_rows)
    relay(0)
    pl.semaphore_wait(credit, len(SHIFTS))
    begin(DX, after=OUT)

    finish(OUT)
    fetch = pltpu.make_async_copy(out_back, dd.at[pl.ds(n_exp, n_exp)], load.at[5])
    fetch.start()
    fetch.wait()
    gg[...] = jnp.zeros_like(gg)

    def combine(_, at):
        pairs = nn(sel_t[...], dd[n_exp : 2 * n_exp, :, at].reshape(rows, at.size))
        p0, p1 = pairs[0:toks], pairs[toks : 2 * toks]
        tok[:, at] = (gate0 * p0 + gate1 * p1).astype(BF16)
        cv = cot[:, at].astype(F32)
        for k, pk in enumerate((p0, p1)):
            prod = cv * pk
            for j in range(0, at.size, 128):
                gg[k] += prod[:, j : j + 128]

    chunks(model, 512, combine)
    mixed_out = pltpu.make_async_copy(tok, mixed, store.at[0])
    mixed_out.start()
    grad_gates[0:1, :] = jnp.sum(gg[0].T, axis=0, keepdims=True)
    grad_gates[1:2, :] = jnp.sum(gg[1].T, axis=0, keepdims=True)
    relay(1)
    relay(2)
    down_out = total(0, grad_d)

    finish(DX)

    def combine_dx(_, at):
        both = sel_t[0:toks, :] + sel_t[toks : 2 * toks, :]
        cot[:, at] = nn(both, xr[:, :, at].reshape(rows, at.size)).astype(BF16)

    chunks(model, 512, combine_dx)
    tok_out = pltpu.make_async_copy(cot, grad_tok, store.at[1])
    tok_out.start()
    gate_out = total(1, grad_g)
    up_out = total(2, grad_u)
    for i in range(len(SHIFTS)):
        block(DX, i).wait_send()
    for kind in range(3):
        for i in range(6):
            ring(kind, i).wait_send()
    for copy in (mixed_out, tok_out, down_out, gate_out, up_out):
        copy.wait()


def per_device(tokens, routes, gates, cotangent, w_gate, w_up, w_down):
    experts, replicas = lax.axis_size("expert"), lax.axis_size("dp")
    toks, model = tokens.shape
    hidden = w_gate.shape[2]
    cap = toks * routes.shape[1] * 3 // (2 * experts)
    rows = experts * cap
    part, fslice = model // replicas, hidden // replicas
    shape = jax.ShapeDtypeStruct
    any_space, vmem = pl.BlockSpec(memory_space=pl.ANY), pl.BlockSpec(memory_space=pltpu.VMEM)
    dma = pltpu.SemaphoreType.DMA
    n = len(SHIFTS)
    outs = pl.pallas_call(
        kernel,
        out_shape=(
            shape((toks, model), BF16),
            shape((toks, model), BF16),
            shape((2, toks), F32),
            shape((1, part, hidden), BF16),
            shape((1, part, hidden), BF16),
            shape((1, fslice, model), BF16),
            shape((experts, cap, model), BF16),
        ),
        in_specs=[vmem, vmem] + [any_space] * 5,
        out_specs=(any_space, any_space, vmem) + (any_space,) * 4,
        scratch_shapes=[
            pltpu.VMEM((toks, model), BF16),
            pltpu.VMEM((toks, model), BF16),
            pltpu.VMEM((model, hidden), BF16),
            pltpu.VMEM((model, hidden), BF16),
            pltpu.VMEM((hidden, model), BF16),
            pltpu.VMEM((rows, toks), BF16),
            pltpu.VMEM((2 * toks, rows), BF16),
            pltpu.VMEM((experts, cap, model), BF16),
            pltpu.VMEM((experts, cap, model), BF16),
            pltpu.VMEM((experts, cap, model), BF16),
            pltpu.VMEM((2 * experts, cap, model), BF16),
            pltpu.VMEM((SIDE, experts, cap, part), BF16),
            pltpu.VMEM((rows, hidden), F32),
            pltpu.VMEM((rows, hidden), F32),
            pltpu.VMEM((rows, hidden), BF16),
            pltpu.VMEM((2 * rows, hidden), BF16),
            pltpu.VMEM((2 * rows, hidden), BF16),
            pltpu.VMEM((2, SIDE, fslice, rows), BF16),
            pltpu.VMEM((SIDE, fslice, rows), BF16),
            pltpu.VMEM((SIDE, part, hidden), BF16),
            pltpu.VMEM((SIDE, part, hidden), BF16),
            pltpu.VMEM((6, part // 2, hidden), BF16),
            pltpu.VMEM((6, part // 2, hidden), BF16),
            pltpu.VMEM((6, fslice // 2, model), BF16),
            pltpu.VMEM((2, toks, 128), F32),
            dma((4, n)),
            dma((4, n)),
            dma((4,)),
            dma((8,)),
            dma((8,)),
            dma((3, 6)),
            dma((3, 6)),
            dma((6,)),
            dma((5,)),
            pltpu.SemaphoreType.REGULAR,
        ],
        compiler_params=pltpu.CompilerParams(
            collective_id=0, has_side_effects=True, vmem_limit_bytes=63 << 20
        ),
        name="expert_layer",
    )(routes.T, gates.T, tokens, cotangent, w_gate, w_up, w_down)
    return (outs[0], outs[1], outs[2].T, outs[3], outs[4], outs[5])


def solution(mesh):
    rows, whole = P(("dp", "expert"), None), P("expert", None, None)
    grads = P("expert", "dp", None)
    return jax.shard_map(
        per_device,
        mesh=mesh,
        in_specs=(rows,) * 4 + (whole,) * 3,
        out_specs=(rows,) * 3 + (grads,) * 3,
        check_vma=False,
    )
```

time: 281 us -> 194 us (0.69)
  Pallas kernels: 0 us -> 180 us
  waiting for transfers between devices: 158 us -> 0 us
  matrix products: 79.2 us -> 0 us
  starting transfers between devices: 21.2 us -> 0 us
  between operations: 13.9 us -> 0.66 us
  local copies, waits for them, and re-layouts: 6.23 us -> 9.71 us
    pallas_call x0 -> x1, Pallas kernels: none -> 180 us  [per_device(): pl.pallas_call(kernel, out_shape=(shape((toks, model), BF16), shape((toks...]
    all_to_all x4 -> x0, waiting for transfers between devices: 148 us -> none  [the longest x1 44.9 us: per_device(): lax.all_to_all(dbuf, 'expert', split_axis=0, concat_axis=0, tiled=True)]
    dot_general x13 -> x0, matrix products: 79.2 us -> none  [the longest x3 23.4 us: contract_rows(): lax.dot_general(left, right, (((0,), (0,)), ((), ())), preferred_element_...]
    all_to_all x4 -> x0, starting transfers between devices: 20.9 us -> none  [the longest x1 7.16 us: per_device(): lax.all_to_all(dbuf, 'expert', split_axis=0, concat_axis=0, tiled=True)]
    reduce_scatter x3 -> x0, waiting for transfers between devices: 10.2 us -> none  [the longest x1 10.2 us: per_device(): lax.psum_scatter(contract_rows(rows_x, d_upv).astype(jnp.bfloat16), 'dp',...]
    unnamed x14 -> x10, local copies, waits for them, and re-layouts: 4.08 us -> 9.71 us
  transfers between devices with their start and end apart: 7 -> 0, of which waited for: 5 -> 0; matrix products, arithmetic and copies ran while one was open for 21% -> 0% of each run, Pallas kernels for 0% -> 0%
where the time goes in v1:
time: 194 us; the launch traced here: 191 us
  Pallas kernels  180 us (93%)
  local copies, waits for them, and re-layouts  9.71 us (5%)
    pallas_call x1, Pallas kernels, per_device(): pl.pallas_call(kernel, out_shape=(shape((toks, model), BF16), shape((toks...  180 us
    unnamed x10, local copies, waits for them, and re-layouts  9.71 us

profile of v1, /device:TPU:0, one launch (start us, length us, event | category | flops | bytes accessed | tf_op | source)
XLA Modules:
  0.0 190.6 jit_solution(16130765261629418181)
XLA Ops:
  0.6 180.2 %expert_layer.1 = (bf16[128,4096]{1,0:T(8,128)(2,1)}, bf16[128,4096]{1,0:T(8,128)(2,1)}, f32[2,128]{1,0:T(2,128)}, bf16[1,512,768]{2,1,0:T(8,128)(2,1)}, bf16[1,...) custom-call(s32[2,128]{1,0:T(2,128)} %bitcast.3, f32[2,128]{1,0:T(2,128)} %bitcast.4, ...), custom_call_target="tpu_custom_call" | custom-call | tf_op jit(solution)/shard_map/expert_layer/pallas_call | solution.py:342
  180.8 0.0 copy-start.1
  180.8 0.0 copy-start
  180.9 2.4 %copy.19 = bf16[128,4096]{1,0:T(8,128)(2,1)} copy(bf16[128,4096]{1,0:T(8,128)(2,1)} %get-tuple-element.24) | data formatting | bytes 2097152
  183.3 2.3 %copy.20 = bf16[128,4096]{1,0:T(8,128)(2,1)} copy(bf16[128,4096]{1,0:T(8,128)(2,1)} %get-tuple-element.25) | data formatting | bytes 2097152
  185.5 1.2 copy.21
  186.7 2.1 %copy.22 = bf16[1,512,768]{2,1,0:T(8,128)(2,1)} copy(bf16[1,512,768]{2,1,0:T(8,128)(2,1)} %get-tuple-element.27) | data formatting | bytes 1572864
  188.8 0.0 copy-done.1
  188.8 0.9 copy.23
  189.7 0.0 copy-done
  189.7 0.9 copy.24
Async XLA Ops:
  180.8 8.0 %copy-start.1 = (bf16[1,512,768]{2,1,0:T(8,128)(2,1)S(1)}, bf16[1,512,768]{2,1,0:T(8,128)(2,1)}, u32[]{:S(2)}) copy-start(bf16[1,512,768]{2,1,0:T(8,128)(2,1)} %get-tuple-element.28) | copy-start | bytes 2359300
  180.8 8.8 %copy-start = (bf16[1,96,4096]{2,1,0:T(8,128)(2,1)S(1)}, bf16[1,96,4096]{2,1,0:T(8,128)(2,1)}, u32[]{:S(2)}) copy-start(bf16[1,96,4096]{2,1,0:T(8,128)(2,1)} %get-tuple-element.29) | copy-start | bytes 2359300

commit v2 on v1

--- a/solution.py
+++ b/solution.py
@@ -9,15 +9,17 @@
 F32, BF16 = jnp.float32, jnp.bfloat16
 SIDE = 4
 GROUPS = (
+    ((1, 3), (3, 1)),
+    ((1, 1), (3, 3)),
+    ((0, 2), (2, 0)),
+    ((2, 2),),
+    ((1, 2), (3, 2), (1, 0), (3, 0)),
     ((2, 1), (2, 3), (0, 1), (0, 3)),
-    ((1, 2), (3, 2), (1, 0), (3, 0)),
-    ((2, 2),),
-    ((0, 2), (2, 0)),
-    ((1, 1), (3, 3)),
-    ((1, 3), (3, 1)),
 )
 SHIFTS = tuple(shift for group in GROUPS for shift in group)
 X, DY, OUT, DX = range(4)
+HALVES = 2
+DOWN, GATE, UP = (0, 1), 2, 3
 
 
 def nn(a, b):
@@ -36,7 +38,7 @@
     routes, gates, tok_in, cot_in, wg_in, wu_in, wd_in,
     mixed, grad_tok, grad_gates, grad_g, grad_u, grad_d, out_back,
     tok, cot, wg, wu, wd, sel, sel_t, buf_a, buf_b, xr, dd, xs, h, u, act, dhc, duc, act_t, act_s, dwg, dwu,
-    zr_g, zr_u, zr_d, gg,
+    zr_g, zr_u, zr_d, dact, gg,
     send, recv, local, sib_send, sib_recv, z_send, z_recv, load, store, credit,
 ):
     n_exp, cap, model = buf_a.shape
@@ -59,7 +61,7 @@
         pltpu.make_async_copy(src, dst, load.at[i])
         for i, (src, dst) in enumerate(((tok_in, tok), (cot_in, cot), (wg_in.at[0], wg), (wu_in.at[0], wu), (wd_in.at[0], wd)))
     ]
-    for copy in loads:
+    for copy in loads[:2]:
         copy.start()
     barrier = pltpu.get_barrier_semaphore()
     for shift in SHIFTS:
@@ -94,58 +96,80 @@
 
     source = (buf_a, buf_b, buf_a, buf_b)
     target = (xr, dd, out_back, xr)
-
-    def block(kind, i):
+    width = model // HALVES
+
+    def columns_of(half):
+        return pl.ds(half * width, width)
+
+    def span(kind, half):
+        return pl.ds(0, model) if kind in (OUT, DX) else columns_of(half)
+
+    def block(kind, half, i):
         to = peer(SHIFTS[i])
         return pltpu.make_async_remote_copy(
-            src_ref=source[kind].at[to], dst_ref=target[kind].at[e],
-            send_sem=send.at[kind, i], recv_sem=recv.at[kind, i],
+            src_ref=source[kind].at[to, :, span(kind, half)], dst_ref=target[kind].at[e, :, span(kind, half)],
+            send_sem=send.at[kind, half, i], recv_sem=recv.at[kind, half, i],
             device_id=(r, to), device_id_type=MESH,
         )
 
-    def arriving(kind, i):
+    def arriving(kind, half, i):
         return pltpu.make_async_remote_copy(
-            src_ref=source[kind].at[e], dst_ref=target[kind].at[peer(SHIFTS[i], -1)],
-            send_sem=send.at[kind, i], recv_sem=recv.at[kind, i],
+            src_ref=source[kind].at[e, :, span(kind, half)],
+            dst_ref=target[kind].at[peer(SHIFTS[i], -1), :, span(kind, half)],
+            send_sem=send.at[kind, half, i], recv_sem=recv.at[kind, half, i],
             device_id=(r, peer(SHIFTS[i])), device_id_type=MESH,
         )
 
-    def own(kind):
-        return pltpu.make_async_copy(source[kind].at[e], target[kind].at[e], local.at[kind])
-
-    def begin(kind, after=None):
-        own(kind).start()
-        first = 0
-        for group in GROUPS:
+    def own(kind, half):
+        return pltpu.make_async_copy(
+            source[kind].at[e, :, span(kind, half)], target[kind].at[e, :, span(kind, half)], local.at[kind, half]
+        )
+
+    def begin(kind, half, after=(), groups=range(len(GROUPS))):
+        if 0 in groups:
+            own(kind, half).start()
+        for g in groups:
+            group = GROUPS[g]
+            first = sum(len(x) for x in GROUPS[:g])
             for i in range(first, first + len(group)):
-                if after is not None:
-                    block(after, i).wait_send()
+                for earlier in after:
+                    block(*earlier, i).wait_send()
             for i in range(first, first + len(group)):
-                block(kind, i).start()
-            first += len(group)
-
-    def finish(kind):
-        own(kind).wait()
+                block(kind, half, i).start()
+
+    def finish(kind, half):
+        own(kind, half).wait()
         for i in range(len(SHIFTS)):
-            arriving(kind, i).wait_recv()
+            arriving(kind, half, i).wait_recv()
+
+    def half_chunks(half, size, body):
+        @pl.loop(0, width // size)
+        def _(i):
+            body(pl.ds(pl.multiple_of(half * width + i * size, size), size))
 
     loads[0].wait()
 
-    def fill_x(_, at):
+    def fill_x(at):
         buf_a[:, :, at] = nn(sel[...], tok[:, at]).astype(BF16).reshape(n_exp, cap, at.size)
 
-    chunks(model, 1024, fill_x)
+    half_chunks(0, 1024, fill_x)
     pl.semaphore_wait(barrier, len(SHIFTS) + 3)
-    begin(X)
+    begin(X, 0)
+    half_chunks(1, 1024, fill_x)
+    begin(X, 1)
+    for copy in loads[2:]:
+        copy.start()
     loads[1].wait()
 
-    def fill_d(_, at):
+    def fill_d(at):
         buf_b[:, :, at] = (nn(sel[...], cot[:, at]) * row_gate).astype(BF16).reshape(n_exp, cap, at.size)
 
-    chunks(model, 1024, fill_d)
-    begin(DY, after=X)
-
-    finish(X)
+    half_chunks(0, 1024, fill_d)
+    half_chunks(1, 1024, fill_d)
+    begin(DY, 0, after=((X, 0), (X, 1)))
+
+    finish(X, 0)
+    finish(X, 1)
     part = model // (2 * SIDE)
 
     def x_part(zz, core):
@@ -186,42 +210,41 @@
         buf_a[:, :, at] = nn(act[...], wd[:, at]).astype(BF16).reshape(n_exp, cap, at.size)
 
     chunks(model, 1024, down_proj)
-    begin(OUT, after=DY)
-
-    finish(DY)
-    sib_d = to_sibling(dd.at[pl.ds(0, n_exp)], dd.at[pl.ds(n_exp, n_exp)], 5)
-    sib_d.start()
-
-    def back_act(_, at):
-        da = nt(dd[0:n_exp].reshape(rows, model), wd[at, :])
-        hv, uv = h[:, at], u[:, at]
-        sg = jax.nn.sigmoid(hv)
-        dhc[0:rows, at] = (da * uv * sg * (1.0 + hv * (1.0 - sg))).astype(BF16)
-        duc[0:rows, at] = (da * hv * sg).astype(BF16)
-
-    chunks(hidden, 256, back_act)
-    sib_dh = to_sibling(dhc.at[pl.ds(0, rows)], dhc.at[pl.ds(rows, rows)], 6)
-    sib_du = to_sibling(duc.at[pl.ds(0, rows)], duc.at[pl.ds(rows, rows)], 7)
-    sib_dh.start()
-    sib_du.start()
-
-    sib_act.wait()
-    sib_d.wait()
-
-    def grad_down(_, at):
+    begin(DY, 1, after=((DY, 0),))
+
+    finish(DY, 0)
+
+    def sib_d(half):
+        return to_sibling(
+            dd.at[pl.ds(0, n_exp), :, columns_of(half)], dd.at[pl.ds(n_exp, n_exp), :, columns_of(half)], 5 + half
+        )
+
+    sib_d(0).start()
+
+    def back_act(half):
+        def body(_, at):
+            dact[:, at] = nt(dd[0:n_exp, :, half * width : (half + 1) * width].reshape(rows, width), wd[at, columns_of(half)])
+
+        return body
+
+    chunks(hidden, 256, back_act(0))
+
+    def grad_down(at):
         left = jnp.concatenate([act_t[c].reshape(SIDE * fslice, rows), act_s[...].reshape(SIDE * fslice, rows)], axis=1)
         wd[0 : SIDE * fslice, at] = nn(left, dd[:, :, at].reshape(2 * rows, at.size)).astype(BF16)
 
-    chunks(model, 512, grad_down)
+    sib_act.wait()
+    sib_d(0).wait()
+    half_chunks(0, 512, grad_down)
 
     half_f, half_p = fslice // 2, part // 2
 
     def half_of(kind, zz, half):
-        if kind == 0:
-            return wd.at[pl.ds(pl.multiple_of(zz * fslice + half * half_f, half_f), half_f)]
-        return (dwg, dwu)[kind - 1].at[zz, pl.ds(half * half_p, half_p)]
-
-    zr = (zr_d, zr_g, zr_u)
+        if kind in DOWN:
+            return wd.at[pl.ds(pl.multiple_of(zz * fslice + half * half_f, half_f), half_f), columns_of(kind)]
+        return (dwg, dwu)[kind - GATE].at[zz, pl.ds(half * half_p, half_p)]
+
+    zr = (zr_d.at[0], zr_d.at[1], zr_g, zr_u)
 
     def hop(kind, i, src, device):
         return pltpu.make_async_remote_copy(
@@ -250,12 +273,36 @@
         for half, (a, b) in enumerate(((2, 5), (3, 4))):
             mine = half_of(kind, z, half)
             mine[...] = (mine[...].astype(F32) + zr[kind][a].astype(F32) + zr[kind][b].astype(F32)).astype(BF16)
-        whole = wd.at[pl.ds(pl.multiple_of(z * fslice, fslice), fslice)] if kind == 0 else (dwg, dwu)[kind - 1].at[z]
-        copy = pltpu.make_async_copy(whole, out.at[0], store.at[2 + kind])
+        if kind in DOWN:
+            whole = wd.at[pl.ds(pl.multiple_of(z * fslice, fslice), fslice), columns_of(kind)]
+            out = out.at[0, :, columns_of(kind)]
+        else:
+            whole, out = (dwg, dwu)[kind - GATE].at[z], out.at[0]
+        copy = pltpu.make_async_copy(whole, out, store.at[2 + kind])
         copy.start()
         return copy
 
-    first_hops(0)
+    first_hops(DOWN[0])
+    begin(OUT, 0, after=((DY, 1),))
+    relay(DOWN[0])
+    finish(DY, 1)
+    sib_d(1).start()
+
+    def back_act_last(_, at):
+        da = dact[:, at] + nt(dd[0:n_exp, :, width:].reshape(rows, width), wd[at, columns_of(1)])
+        hv, uv = h[:, at], u[:, at]
+        sg = jax.nn.sigmoid(hv)
+        dhc[0:rows, at] = (da * uv * sg * (1.0 + hv * (1.0 - sg))).astype(BF16)
+        duc[0:rows, at] = (da * hv * sg).astype(BF16)
+
+    chunks(hidden, 256, back_act_last)
+    sib_dh = to_sibling(dhc.at[pl.ds(0, rows)], dhc.at[pl.ds(rows, rows)], 7)
+    sib_du = to_sibling(duc.at[pl.ds(0, rows)], duc.at[pl.ds(rows, rows)], 8)
+    sib_dh.start()
+    sib_du.start()
+    sib_d(1).wait()
+    half_chunks(1, 512, grad_down)
+    first_hops(DOWN[1])
     for copy in sib_x:
         copy.wait()
 
@@ -268,10 +315,10 @@
 
     sib_dh.wait()
     grad_in(dhc, dwg)
-    first_hops(1)
+    first_hops(GATE)
     sib_du.wait()
     grad_in(duc, dwu)
-    first_hops(2)
+    first_hops(UP)
     for i in range(len(SHIFTS)):
         pl.semaphore_signal(credit, inc=1, device_id=(r, peer(SHIFTS[i])), device_id_type=MESH)
 
@@ -279,11 +326,11 @@
         buf_b[:, :, at] = (nt(dhc[0:rows], wg[at, :]) + nt(duc[0:rows], wu[at, :])).astype(BF16).reshape(n_exp, cap, at.size)
 
     chunks(model, 512, back_rows)
-    relay(0)
+    relay(DOWN[1])
     pl.semaphore_wait(credit, len(SHIFTS))
-    begin(DX, after=OUT)
-
-    finish(OUT)
+    begin(DX, 0, after=((OUT, 0),))
+
+    finish(OUT, 0)
     fetch = pltpu.make_async_copy(out_back, dd.at[pl.ds(n_exp, n_exp)], load.at[5])
     fetch.start()
     fetch.wait()
@@ -304,27 +351,39 @@
     mixed_out.start()
     grad_gates[0:1, :] = jnp.sum(gg[0].T, axis=0, keepdims=True)
     grad_gates[1:2, :] = jnp.sum(gg[1].T, axis=0, keepdims=True)
-    relay(1)
-    relay(2)
-    down_out = total(0, grad_d)
-
-    finish(DX)
-
-    def combine_dx(_, at):
+    relay(GATE)
+    relay(UP)
+    stores = [mixed_out] + [total(kind, grad_d) for kind in DOWN]
+
+    def combine_dx(at):
         both = sel_t[0:toks, :] + sel_t[toks : 2 * toks, :]
         cot[:, at] = nn(both, xr[:, :, at].reshape(rows, at.size)).astype(BF16)
 
-    chunks(model, 512, combine_dx)
-    tok_out = pltpu.make_async_copy(cot, grad_tok, store.at[1])
-    tok_out.start()
-    gate_out = total(1, grad_g)
-    up_out = total(2, grad_u)
+    finish(DX, 0)
+    chunks(model, 512, lambda _, at: combine_dx(at))
+    stores.append(pltpu.make_async_copy(cot, grad_tok, store.at[1]))
+    stores[-1].start()
+    stores += [total(GATE, grad_g), total(UP, grad_u)]
     for i in range(len(SHIFTS)):
-        block(DX, i).wait_send()
-    for kind in range(3):
+        block(DX, 0, i).wait_send()
+    for kind in (*DOWN, GATE, UP):
         for i in range(6):
             ring(kind, i).wait_send()
-    for copy in (mixed_out, tok_out, down_out, gate_out, up_out):
+    for copy in stores:
+        copy.wait()
+
+
+def copy_out(*refs):
+    n = len(refs) // 3
+    ins, outs, held, (load, store) = refs[:n], refs[n : 2 * n], refs[2 * n : 3 * n], refs[3 * n :]
+    loads = [pltpu.make_async_copy(ins[i], held[i], load.at[i]) for i in range(n)]
+    stores = [pltpu.make_async_copy(held[i], outs[i], store.at[i]) for i in range(n)]
+    for copy in loads:
+        copy.start()
+    for first, second in zip(loads, stores):
+        first.wait()
+        second.start()
+    for copy in stores:
         copy.wait()
 
 
@@ -376,17 +435,18 @@
             pltpu.VMEM((SIDE, part, hidden), BF16),
             pltpu.VMEM((6, part // 2, hidden), BF16),
             pltpu.VMEM((6, part // 2, hidden), BF16),
-            pltpu.VMEM((6, fslice // 2, model), BF16),
+            pltpu.VMEM((2, 6, fslice // 2, model // 2), BF16),
+            pltpu.VMEM((rows, hidden), F32),
             pltpu.VMEM((2, toks, 128), F32),
-            dma((4, n)),
-            dma((4, n)),
-            dma((4,)),
-            dma((8,)),
-            dma((8,)),
-            dma((3, 6)),
-            dma((3, 6)),
+            dma((4, HALVES, n)),
+            dma((4, HALVES, n)),
+            dma((4, HALVES)),
+            dma((9,)),
+            dma((9,)),
+            dma((4, 6)),
+            dma((4, 6)),
             dma((6,)),
-            dma((5,)),
+            dma((6,)),
             pltpu.SemaphoreType.REGULAR,
         ],
         compiler_params=pltpu.CompilerParams(
@@ -394,6 +454,16 @@
         ),
         name="expert_layer",
     )(routes.T, gates.T, tokens, cotangent, w_gate, w_up, w_down)
+    outs = outs[:6]
+    outs = pl.pallas_call(
+        copy_out,
+        out_shape=tuple(shape(o.shape, o.dtype) for o in outs),
+        in_specs=[any_space] * len(outs),
+        out_specs=(any_space,) * len(outs),
+        scratch_shapes=[pltpu.VMEM(o.shape, o.dtype) for o in outs] + [dma((len(outs),))] * 2,
+        compiler_params=pltpu.CompilerParams(vmem_limit_bytes=60 << 20),
+        name="copy_out",
+    )(*outs)
     return (outs[0], outs[1], outs[2].T, outs[3], outs[4], outs[5])
 
 

time: 194 us -> 171 us (0.88)
  the two profiles are of different devices: /device:TPU:0 before, /device:TPU:38 now
where the time goes in v2:
time: 171 us; the launch traced here: 170 us
  Pallas kernels  170 us (99%)
    pallas_call x1, Pallas kernels, per_device(): pl.pallas_call(kernel, out_shape=(shape((toks, model), BF16), shape((toks...  166 us
    pallas_call x1, Pallas kernels, per_device(): pl.pallas_call(copy_out, out_shape=tuple((shape(o.shape, o.dtype) for o i...  3.49 us

profile of v2, /device:TPU:38, one launch (start us, length us, event | category | flops | bytes accessed | tf_op | source)
XLA Modules:
  0.0 170.4 jit_solution(9636697657988813059)
XLA Ops:
  0.6 166.2 %expert_layer.1 = (bf16[128,4096]{1,0:T(8,128)(2,1)}, bf16[128,4096]{1,0:T(8,128)(2,1)}, f32[2,128]{1,0:T(2,128)}, bf16[1,512,768]{2,1,0:T(8,128)(2,1)}, bf16[1,...) custom-call(s32[2,128]{1,0:T(2,128)} %bitcast.3, f32[2,128]{1,0:T(2,128)} %bitcast.4, ...), custom_call_target="tpu_custom_call" | custom-call | tf_op jit(solution)/shard_map/expert_layer/pallas_call | solution.py:401
  166.9 3.5 %copy_out.1 = (bf16[128,4096]{1,0:T(8,128)(2,1)}, bf16[128,4096]{1,0:T(8,128)(2,1)}, f32[2,128]{1,0:T(2,128)}, bf16[1,512,768]{2,1,0:T(8,128)(2,1)}, bf16[1,512,...) custom-call(bf16[128,4096]{1,0:T(8,128)(2,1)} %get-tuple-element.18.refs_0_, ...), custom_call_target="tpu_custom_call" | custom-call | tf_op jit(solution)/shard_map/copy_out/pallas_call | solution.py:458

commit v3 on v2

--- a/solution.py
+++ b/solution.py
@@ -101,28 +101,25 @@
     def columns_of(half):
         return pl.ds(half * width, width)
 
-    def span(kind, half):
-        return pl.ds(0, model) if kind in (OUT, DX) else columns_of(half)
-
     def block(kind, half, i):
         to = peer(SHIFTS[i])
         return pltpu.make_async_remote_copy(
-            src_ref=source[kind].at[to, :, span(kind, half)], dst_ref=target[kind].at[e, :, span(kind, half)],
+            src_ref=source[kind].at[to, :, columns_of(half)], dst_ref=target[kind].at[e, :, columns_of(half)],
             send_sem=send.at[kind, half, i], recv_sem=recv.at[kind, half, i],
             device_id=(r, to), device_id_type=MESH,
         )
 
     def arriving(kind, half, i):
         return pltpu.make_async_remote_copy(
-            src_ref=source[kind].at[e, :, span(kind, half)],
-            dst_ref=target[kind].at[peer(SHIFTS[i], -1), :, span(kind, half)],
+            src_ref=source[kind].at[e, :, columns_of(half)],
+            dst_ref=target[kind].at[peer(SHIFTS[i], -1), :, columns_of(half)],
             send_sem=send.at[kind, half, i], recv_sem=recv.at[kind, half, i],
             device_id=(r, peer(SHIFTS[i])), device_id_type=MESH,
         )
 
     def own(kind, half):
         return pltpu.make_async_copy(
-            source[kind].at[e, :, span(kind, half)], target[kind].at[e, :, span(kind, half)], local.at[kind, half]
+            source[kind].at[e, :, columns_of(half)], target[kind].at[e, :, columns_of(half)], local.at[kind, half]
         )
 
     def begin(kind, half, after=(), groups=range(len(GROUPS))):
@@ -284,6 +281,7 @@
 
     first_hops(DOWN[0])
     begin(OUT, 0, after=((DY, 1),))
+    begin(OUT, 1)
     relay(DOWN[0])
     finish(DY, 1)
     sib_d(1).start()
@@ -328,9 +326,10 @@
     chunks(model, 512, back_rows)
     relay(DOWN[1])
     pl.semaphore_wait(credit, len(SHIFTS))
-    begin(DX, 0, after=((OUT, 0),))
+    begin(DX, 0, after=((OUT, 0), (OUT, 1)))
 
     finish(OUT, 0)
+    finish(OUT, 1)
     fetch = pltpu.make_async_copy(out_back, dd.at[pl.ds(n_exp, n_exp)], load.at[5])
     fetch.start()
     fetch.wait()
@@ -352,6 +351,7 @@
     grad_gates[0:1, :] = jnp.sum(gg[0].T, axis=0, keepdims=True)
     grad_gates[1:2, :] = jnp.sum(gg[1].T, axis=0, keepdims=True)
     relay(GATE)
+    begin(DX, 1, after=((DX, 0),))
     relay(UP)
     stores = [mixed_out] + [total(kind, grad_d) for kind in DOWN]
 
@@ -360,12 +360,13 @@
         cot[:, at] = nn(both, xr[:, :, at].reshape(rows, at.size)).astype(BF16)
 
     finish(DX, 0)
+    finish(DX, 1)
     chunks(model, 512, lambda _, at: combine_dx(at))
     stores.append(pltpu.make_async_copy(cot, grad_tok, store.at[1]))
     stores[-1].start()
     stores += [total(GATE, grad_g), total(UP, grad_u)]
     for i in range(len(SHIFTS)):
-        block(DX, 0, i).wait_send()
+        block(DX, 1, i).wait_send()
     for kind in (*DOWN, GATE, UP):
         for i in range(6):
             ring(kind, i).wait_send()

time: 171 us -> 163 us (0.953)
  the two profiles are of different devices: /device:TPU:38 before, /device:TPU:0 now
where the time goes in v3:
time: 163 us; the launch traced here: 161 us
  Pallas kernels  160 us (98%)
    pallas_call x1, Pallas kernels, per_device(): pl.pallas_call(kernel, out_shape=(shape((toks, model), BF16), shape((toks...  157 us
    pallas_call x1, Pallas kernels, per_device(): pl.pallas_call(copy_out, out_shape=tuple((shape(o.shape, o.dtype) for o i...  3.49 us

profile of v3, /device:TPU:0, one launch (start us, length us, event | category | flops | bytes accessed | tf_op | source)
XLA Modules:
  0.0 160.6 jit_solution(5896068386468836385)
XLA Ops:
  0.6 156.5 %expert_layer.1 = (bf16[128,4096]{1,0:T(8,128)(2,1)}, bf16[128,4096]{1,0:T(8,128)(2,1)}, f32[2,128]{1,0:T(2,128)}, bf16[1,512,768]{2,1,0:T(8,128)(2,1)}, bf16[1,...) custom-call(s32[2,128]{1,0:T(2,128)} %bitcast.3, f32[2,128]{1,0:T(2,128)} %bitcast.4, ...), custom_call_target="tpu_custom_call" | custom-call | tf_op jit(solution)/shard_map/expert_layer/pallas_call | solution.py:402
  157.2 3.5 %copy_out.1 = (bf16[128,4096]{1,0:T(8,128)(2,1)}, bf16[128,4096]{1,0:T(8,128)(2,1)}, f32[2,128]{1,0:T(2,128)}, bf16[1,512,768]{2,1,0:T(8,128)(2,1)}, bf16[1,512,...) custom-call(bf16[128,4096]{1,0:T(8,128)(2,1)} %get-tuple-element.18.refs_0_, ...), custom_call_target="tpu_custom_call" | custom-call | tf_op jit(solution)/shard_map/copy_out/pallas_call | solution.py:459

commit v4 on v3

--- a/solution.py
+++ b/solution.py
@@ -18,8 +18,8 @@
 )
 SHIFTS = tuple(shift for group in GROUPS for shift in group)
 X, DY, OUT, DX = range(4)
-HALVES = 2
-DOWN, GATE, UP = (0, 1), 2, 3
+PARTS = (2, 4, 2, 2)
+DOWN, GATE, UP = (0, 1, 2, 3), 4, 5
 
 
 def nn(a, b):
@@ -96,30 +96,30 @@
 
     source = (buf_a, buf_b, buf_a, buf_b)
     target = (xr, dd, out_back, xr)
-    width = model // HALVES
-
-    def columns_of(half):
+
+    def columns_of(kind, half):
+        width = model // PARTS[kind]
         return pl.ds(half * width, width)
 
     def block(kind, half, i):
         to = peer(SHIFTS[i])
         return pltpu.make_async_remote_copy(
-            src_ref=source[kind].at[to, :, columns_of(half)], dst_ref=target[kind].at[e, :, columns_of(half)],
+            src_ref=source[kind].at[to, :, columns_of(kind, half)], dst_ref=target[kind].at[e, :, columns_of(kind, half)],
             send_sem=send.at[kind, half, i], recv_sem=recv.at[kind, half, i],
             device_id=(r, to), device_id_type=MESH,
         )
 
     def arriving(kind, half, i):
         return pltpu.make_async_remote_copy(
-            src_ref=source[kind].at[e, :, columns_of(half)],
-            dst_ref=target[kind].at[peer(SHIFTS[i], -1), :, columns_of(half)],
+            src_ref=source[kind].at[e, :, columns_of(kind, half)],
+            dst_ref=target[kind].at[peer(SHIFTS[i], -1), :, columns_of(kind, half)],
             send_sem=send.at[kind, half, i], recv_sem=recv.at[kind, half, i],
             device_id=(r, peer(SHIFTS[i])), device_id_type=MESH,
         )
 
     def own(kind, half):
         return pltpu.make_async_copy(
-            source[kind].at[e, :, columns_of(half)], target[kind].at[e, :, columns_of(half)], local.at[kind, half]
+            source[kind].at[e, :, columns_of(kind, half)], target[kind].at[e, :, columns_of(kind, half)], local.at[kind, half]
         )
 
     def begin(kind, half, after=(), groups=range(len(GROUPS))):
@@ -139,7 +139,9 @@
         for i in range(len(SHIFTS)):
             arriving(kind, half, i).wait_recv()
 
-    def half_chunks(half, size, body):
+    def part_chunks(kind, half, size, body):
+        width = model // PARTS[kind]
+
         @pl.loop(0, width // size)
         def _(i):
             body(pl.ds(pl.multiple_of(half * width + i * size, size), size))
@@ -149,10 +151,10 @@
     def fill_x(at):
         buf_a[:, :, at] = nn(sel[...], tok[:, at]).astype(BF16).reshape(n_exp, cap, at.size)
 
-    half_chunks(0, 1024, fill_x)
+    part_chunks(X, 0, 1024, fill_x)
     pl.semaphore_wait(barrier, len(SHIFTS) + 3)
     begin(X, 0)
-    half_chunks(1, 1024, fill_x)
+    part_chunks(X, 1, 1024, fill_x)
     begin(X, 1)
     for copy in loads[2:]:
         copy.start()
@@ -161,9 +163,9 @@
     def fill_d(at):
         buf_b[:, :, at] = (nn(sel[...], cot[:, at]) * row_gate).astype(BF16).reshape(n_exp, cap, at.size)
 
-    half_chunks(0, 1024, fill_d)
-    half_chunks(1, 1024, fill_d)
+    chunks(model, 1024, lambda _, at: fill_d(at))
     begin(DY, 0, after=((X, 0), (X, 1)))
+    begin(DY, 1)
 
     finish(X, 0)
     finish(X, 1)
@@ -193,6 +195,7 @@
         act[:, at] = (hv * jax.nn.sigmoid(hv) * uv).astype(BF16)
 
     chunks(hidden, 256, up_proj)
+    begin(DY, 2, after=((DY, 0),))
     fslice = hidden // (2 * SIDE)
     for half in range(2):
         piece = act[:, half * SIDE * fslice : (half + 1) * SIDE * fslice].astype(F32).T.astype(BF16)
@@ -207,41 +210,15 @@
         buf_a[:, :, at] = nn(act[...], wd[:, at]).astype(BF16).reshape(n_exp, cap, at.size)
 
     chunks(model, 1024, down_proj)
-    begin(DY, 1, after=((DY, 0),))
-
-    finish(DY, 0)
-
-    def sib_d(half):
-        return to_sibling(
-            dd.at[pl.ds(0, n_exp), :, columns_of(half)], dd.at[pl.ds(n_exp, n_exp), :, columns_of(half)], 5 + half
-        )
-
-    sib_d(0).start()
-
-    def back_act(half):
-        def body(_, at):
-            dact[:, at] = nt(dd[0:n_exp, :, half * width : (half + 1) * width].reshape(rows, width), wd[at, columns_of(half)])
-
-        return body
-
-    chunks(hidden, 256, back_act(0))
-
-    def grad_down(at):
-        left = jnp.concatenate([act_t[c].reshape(SIDE * fslice, rows), act_s[...].reshape(SIDE * fslice, rows)], axis=1)
-        wd[0 : SIDE * fslice, at] = nn(left, dd[:, :, at].reshape(2 * rows, at.size)).astype(BF16)
-
-    sib_act.wait()
-    sib_d(0).wait()
-    half_chunks(0, 512, grad_down)
 
     half_f, half_p = fslice // 2, part // 2
 
     def half_of(kind, zz, half):
         if kind in DOWN:
-            return wd.at[pl.ds(pl.multiple_of(zz * fslice + half * half_f, half_f), half_f), columns_of(kind)]
+            return wd.at[pl.ds(pl.multiple_of(zz * fslice + half * half_f, half_f), half_f), columns_of(DY, kind)]
         return (dwg, dwu)[kind - GATE].at[zz, pl.ds(half * half_p, half_p)]
 
-    zr = (zr_d.at[0], zr_d.at[1], zr_g, zr_u)
+    zr = (*(zr_d.at[i] for i in DOWN), zr_g, zr_u)
 
     def hop(kind, i, src, device):
         return pltpu.make_async_remote_copy(
@@ -271,36 +248,65 @@
             mine = half_of(kind, z, half)
             mine[...] = (mine[...].astype(F32) + zr[kind][a].astype(F32) + zr[kind][b].astype(F32)).astype(BF16)
         if kind in DOWN:
-            whole = wd.at[pl.ds(pl.multiple_of(z * fslice, fslice), fslice), columns_of(kind)]
-            out = out.at[0, :, columns_of(kind)]
+            whole = wd.at[pl.ds(pl.multiple_of(z * fslice, fslice), fslice), columns_of(DY, kind)]
+            out = out.at[0, :, columns_of(DY, kind)]
         else:
             whole, out = (dwg, dwu)[kind - GATE].at[z], out.at[0]
         copy = pltpu.make_async_copy(whole, out, store.at[2 + kind])
         copy.start()
         return copy
 
-    first_hops(DOWN[0])
-    begin(OUT, 0, after=((DY, 1),))
-    begin(OUT, 1)
-    relay(DOWN[0])
-    finish(DY, 1)
-    sib_d(1).start()
+    def sib_d(half):
+        at = columns_of(DY, half)
+        return to_sibling(dd.at[pl.ds(0, n_exp), :, at], dd.at[pl.ds(n_exp, n_exp), :, at], 5 + half)
+
+    def back_act(half):
+        at = columns_of(DY, half)
+        return lambda f: nt(dd[0:n_exp, :, at].reshape(rows, at.size), wd[f, at])
+
+    def grad_down(at):
+        left = jnp.concatenate([act_t[c].reshape(SIDE * fslice, rows), act_s[...].reshape(SIDE * fslice, rows)], axis=1)
+        wd[0 : SIDE * fslice, at] = nn(left, dd[:, :, at].reshape(2 * rows, at.size)).astype(BF16)
+
+    last = PARTS[DY] - 1
+    sib_act.wait()
+    for half in range(last):
+        finish(DY, half)
+        sib_d(half).start()
+        term = back_act(half)
+
+        def add_act(_, f, half=half, term=term):
+            dact[:, f] = term(f) if half == 0 else dact[:, f] + term(f)
+
+        chunks(hidden, 256, add_act)
+        sib_d(half).wait()
+        part_chunks(DY, half, 512, grad_down)
+        first_hops(DOWN[half])
+        if half + 3 <= last:
+            begin(DY, half + 3, after=((DY, half + 1),))
+        else:
+            begin(OUT, half + 3 - PARTS[DY], after=((DY, half + 1),))
+        if half > 0:
+            relay(DOWN[half - 1])
+    finish(DY, last)
+    sib_d(last).start()
 
     def back_act_last(_, at):
-        da = dact[:, at] + nt(dd[0:n_exp, :, width:].reshape(rows, width), wd[at, columns_of(1)])
+        da = dact[:, at] + back_act(last)(at)
         hv, uv = h[:, at], u[:, at]
         sg = jax.nn.sigmoid(hv)
         dhc[0:rows, at] = (da * uv * sg * (1.0 + hv * (1.0 - sg))).astype(BF16)
         duc[0:rows, at] = (da * hv * sg).astype(BF16)
 
     chunks(hidden, 256, back_act_last)
-    sib_dh = to_sibling(dhc.at[pl.ds(0, rows)], dhc.at[pl.ds(rows, rows)], 7)
-    sib_du = to_sibling(duc.at[pl.ds(0, rows)], duc.at[pl.ds(rows, rows)], 8)
+    sib_dh = to_sibling(dhc.at[pl.ds(0, rows)], dhc.at[pl.ds(rows, rows)], 9)
+    sib_du = to_sibling(duc.at[pl.ds(0, rows)], duc.at[pl.ds(rows, rows)], 10)
     sib_dh.start()
     sib_du.start()
-    sib_d(1).wait()
-    half_chunks(1, 512, grad_down)
-    first_hops(DOWN[1])
+    sib_d(last).wait()
+    part_chunks(DY, last, 512, grad_down)
+    first_hops(DOWN[last])
+    relay(DOWN[last - 1])
     for copy in sib_x:
         copy.wait()
 
@@ -324,7 +330,7 @@
         buf_b[:, :, at] = (nt(dhc[0:rows], wg[at, :]) + nt(duc[0:rows], wu[at, :])).astype(BF16).reshape(n_exp, cap, at.size)
 
     chunks(model, 512, back_rows)
-    relay(DOWN[1])
+    relay(DOWN[last])
     pl.semaphore_wait(credit, len(SHIFTS))
     begin(DX, 0, after=((OUT, 0), (OUT, 1)))
 
@@ -360,8 +366,9 @@
         cot[:, at] = nn(both, xr[:, :, at].reshape(rows, at.size)).astype(BF16)
 
     finish(DX, 0)
+    part_chunks(DX, 0, 512, combine_dx)
     finish(DX, 1)
-    chunks(model, 512, lambda _, at: combine_dx(at))
+    part_chunks(DX, 1, 512, combine_dx)
     stores.append(pltpu.make_async_copy(cot, grad_tok, store.at[1]))
     stores[-1].start()
     stores += [total(GATE, grad_g), total(UP, grad_u)]
@@ -436,18 +443,18 @@
             pltpu.VMEM((SIDE, part, hidden), BF16),
             pltpu.VMEM((6, part // 2, hidden), BF16),
             pltpu.VMEM((6, part // 2, hidden), BF16),
-            pltpu.VMEM((2, 6, fslice // 2, model // 2), BF16),
+            pltpu.VMEM((PARTS[DY], 6, fslice // 2, model // PARTS[DY]), BF16),
             pltpu.VMEM((rows, hidden), F32),
             pltpu.VMEM((2, toks, 128), F32),
-            dma((4, HALVES, n)),
-            dma((4, HALVES, n)),
-            dma((4, HALVES)),
-            dma((9,)),
-            dma((9,)),
-            dma((4, 6)),
-            dma((4, 6)),
+            dma((4, max(PARTS), n)),
+            dma((4, max(PARTS), n)),
+            dma((4, max(PARTS))),
+            dma((11,)),
+            dma((11,)),
+            dma((6, 6)),
+            dma((6, 6)),
             dma((6,)),
-            dma((6,)),
+            dma((8,)),
             pltpu.SemaphoreType.REGULAR,
         ],
         compiler_params=pltpu.CompilerParams(

time: 163 us -> 162 us (level); the launches traced: 161 us -> 162 us
  no operation moved by 1% of the time
where the time goes in v4:
time: 162 us
  Pallas kernels  161 us (99%)
    pallas_call x1, Pallas kernels, per_device(): pl.pallas_call(kernel, out_shape=(shape((toks, model), BF16), shape((toks...  157 us
    pallas_call x1, Pallas kernels, per_device(): pl.pallas_call(copy_out, out_shape=tuple((shape(o.shape, o.dtype) for o i...  3.49 us

profile of v4, /device:TPU:0, one launch (start us, length us, event | category | flops | bytes accessed | tf_op | source)
XLA Modules:
  0.0 161.5 jit_solution(7761421760429334531)
XLA Ops:
  0.6 157.4 %expert_layer.1 = (bf16[128,4096]{1,0:T(8,128)(2,1)}, bf16[128,4096]{1,0:T(8,128)(2,1)}, f32[2,128]{1,0:T(2,128)}, bf16[1,512,768]{2,1,0:T(8,128)(2,1)}, bf16[1,...) custom-call(s32[2,128]{1,0:T(2,128)} %bitcast.3, f32[2,128]{1,0:T(2,128)} %bitcast.4, ...), custom_call_target="tpu_custom_call" | custom-call | tf_op jit(solution)/shard_map/expert_layer/pallas_call | solution.py:409
  158.1 3.5 %copy_out.1 = (bf16[128,4096]{1,0:T(8,128)(2,1)}, bf16[128,4096]{1,0:T(8,128)(2,1)}, f32[2,128]{1,0:T(2,128)}, bf16[1,512,768]{2,1,0:T(8,128)(2,1)}, bf16[1,512,...) custom-call(bf16[128,4096]{1,0:T(8,128)(2,1)} %get-tuple-element.18.refs_0_, ...), custom_call_target="tpu_custom_call" | custom-call | tf_op jit(solution)/shard_map/copy_out/pallas_call | solution.py:466
